TPU v7x, 768 devices: a whole 4x8x12 slice. The times are simulated.
768 devices in a mesh: obs: 96 (over y, z), grid: 8 (over x, core).
Axes of the slice: x: 4, y: 8, z: 12, core: 2. Of those that a mesh axis runs over, the one named last changes fastest.
Arguments:
- queries: bfloat16 [196608, 1024], P(('obs', 'grid')), may hold values from -48 to 48
- latent_kv: bfloat16 [8, 384, 2048], P('grid'), may hold values from -4 to 4
- pair_blocks: int32 [1536, 4], P(('obs', 'grid')), may hold values from 0 to 23, as said below
- pair_count: int32 [1536], P(('obs', 'grid')), may hold values from 1 to 4
- obs_count: int32 [1536], P(('obs', 'grid')), may hold values from 32 to 128
- cotangent: bfloat16 [196608, 1024], P(('obs', 'grid')), may hold values from -6 to 6
Outputs:
- attended: bfloat16 [196608, 1024], P(('obs', 'grid'))
- grad_query: bfloat16 [196608, 1024], P(('obs', 'grid'))
- grad_kv: float32 [8, 384, 2048], P('grid', 'obs')
Inputs may be any that keep to these rules, and one draw needn't show every extreme that they name: `pair_blocks`: obs block n lies in region (n // 2) % 8. Each entry names a patch block b of that region (b // 3 equal to it), or the last patch block of the region before it, or the first patch block of the region after it, regions counted cyclically. Entries of one obs block may repeat.
All inputs are finite; a program needn't handle non-finite values.
Results may differ from a plain program's by a relative error of at most 0.012.
Values may be sent and summed in bfloat16 or wider, within the bound.
A program may use at most 64 MiB of HBM per device.

v0:
```python
import math

import jax
import jax.numpy as jnp
from jax import lax
from jax.sharding import PartitionSpec as P

H = 16


def with_halo(shard, sides, width):
    for axis, dim in sides:
        devices, length = (lax.axis_size(axis), shard.shape[dim])
        up = [(i, (i + 1) % devices) for i in range(devices)]
        down = [(j, i) for i, j in up]
        last = lax.slice_in_dim(shard, length - width, length, axis=dim)
        first = lax.slice_in_dim(shard, 0, width, axis=dim)
        before = lax.ppermute(last, axis, up)
        after = lax.ppermute(first, axis, down)
        shard = jnp.concatenate([before, shard, after], axis=dim)
    return shard


def shifted(block, axis, distance):
    devices = range(lax.axis_size(axis))
    route = [((i - distance) % len(devices), i) for i in devices]
    return lax.ppermute(block, axis, route)


def block_pass(query_rows, kv_rows, key_valid, row_valid, grad_rows):
    feature_count = query_rows.shape[-1]
    head_dim = feature_count // H
    score_scale = 1.0 / math.sqrt(head_dim)
    query_heads = query_rows.reshape(query_rows.shape[0], H, head_dim)
    key_heads = kv_rows[:, :feature_count].reshape(kv_rows.shape[0], H, head_dim)
    value_heads = kv_rows[:, feature_count:].reshape(kv_rows.shape[0], H, head_dim)
    scores = (
        jnp.einsum("qhd,khd->hqk", query_heads, key_heads, preferred_element_type=jnp.float32)
        * score_scale
    )
    scores = jnp.where(key_valid[None, None, :], scores, -1e30)
    row_max = jnp.max(scores, axis=-1, keepdims=True)
    expanded = jnp.exp(scores - row_max)
    attention = expanded / jnp.sum(expanded, axis=-1, keepdims=True)
    attention_low = attention.astype(jnp.bfloat16)
    mixed = jnp.einsum(
        "hqk,khd->qhd", attention_low, value_heads, preferred_element_type=jnp.float32
    )
    mixed = mixed.reshape(query_rows.shape[0], feature_count)
    attended = jnp.where(row_valid[:, None], mixed, 0.0).astype(jnp.bfloat16)
    grad_heads = jnp.where(row_valid[:, None], grad_rows, 0).reshape(query_heads.shape)
    grad_values = jnp.einsum(
        "hqk,qhd->khd", attention_low, grad_heads, preferred_element_type=jnp.float32
    )
    grad_attention = jnp.einsum(
        "qhd,khd->hqk", grad_heads, value_heads, preferred_element_type=jnp.float32
    )
    delta_term = jnp.sum(attention * grad_attention, axis=-1, keepdims=True)
    grad_low = (attention * (grad_attention - delta_term) * score_scale).astype(jnp.bfloat16)
    grad_query = jnp.einsum("hqk,khd->qhd", grad_low, key_heads, preferred_element_type=jnp.float32)
    grad_query = grad_query.reshape(query_rows.shape[0], feature_count).astype(jnp.bfloat16)
    grad_keys = jnp.einsum(
        "hqk,qhd->khd", grad_low, query_heads, preferred_element_type=jnp.float32
    )
    grad_kv = jnp.concatenate(
        [
            grad_keys.reshape(kv_rows.shape[0], feature_count),
            grad_values.reshape(kv_rows.shape[0], feature_count),
        ],
        axis=1,
    )
    return (attended, grad_query, grad_kv)


def per_device(queries, latent_kv, pair_blocks, pair_count, obs_count, cotangent):
    block_count, slot_count = pair_blocks.shape
    row_total, feature_count = queries.shape
    block_rows = row_total // block_count
    own_latent = latent_kv[0]
    latent_rows = own_latent.shape[0]
    latent_blocks = latent_rows // block_rows
    region = lax.axis_index("grid")
    region_count = lax.axis_size("grid")
    window = with_halo(own_latent, (("grid", 0),), block_rows)
    window_blocks = window.reshape(latent_blocks + 2, block_rows, 2 * feature_count)
    owner_region = pair_blocks // latent_blocks
    offset = (owner_region - region) % region_count
    window_slot = jnp.where(
        offset == 0, pair_blocks % latent_blocks + 1, jnp.where(offset == 1, latent_blocks + 1, 0)
    )
    slot_rows = jnp.arange(slot_count * block_rows, dtype=jnp.int32) // block_rows
    row_index = jnp.arange(block_rows, dtype=jnp.int32)

    def advance(grad_window, inputs):
        query_rows, slot_ids, live_pairs, live_rows, grad_rows = inputs
        kv_rows = window_blocks[slot_ids].reshape(slot_count * block_rows, 2 * feature_count)
        attended, grad_query, grad_kv = block_pass(
            query_rows, kv_rows, slot_rows < live_pairs, row_index < live_rows, grad_rows
        )
        grad_window = grad_window.at[slot_ids].add(
            grad_kv.reshape(slot_count, block_rows, 2 * feature_count)
        )
        return (grad_window, (attended, grad_query))

    initial = jnp.zeros((latent_blocks + 2, block_rows, 2 * feature_count), jnp.float32)
    scanned = (
        queries.reshape(block_count, block_rows, feature_count),
        window_slot,
        pair_count,
        obs_count,
        cotangent.reshape(block_count, block_rows, feature_count),
    )
    grad_window, (attended, grad_query) = lax.scan(advance, initial, scanned)
    grad_window = grad_window.reshape((latent_blocks + 2) * block_rows, 2 * feature_count)
    lower_rim = grad_window[:block_rows]
    middle = grad_window[block_rows : block_rows + latent_rows]
    upper_rim = grad_window[block_rows + latent_rows :]
    from_after = shifted(lower_rim, "grid", -1)
    from_before = shifted(upper_rim.astype(jnp.bfloat16), "grid", 1).astype(upper_rim.dtype)
    middle = middle.at[:block_rows].add(from_before).at[latent_rows - block_rows :].add(from_after)
    summed = lax.psum_scatter(middle, "obs", scatter_dimension=0, tiled=True)
    return (
        attended.reshape(row_total, feature_count),
        grad_query.reshape(row_total, feature_count),
        summed[None],
    )


def solution(mesh):
    placed = (
        P(("obs", "grid"), None),
        P("grid", None, None),
        P(("obs", "grid"), None),
        P(("obs", "grid")),
        P(("obs", "grid")),
        P(("obs", "grid"), None),
    )
    return jax.shard_map(
        per_device,
        mesh=mesh,
        in_specs=placed,
        out_specs=(P(("obs", "grid"), None), P(("obs", "grid"), None), P("grid", "obs", None)),
        check_vma=False,
    )
```

profile of v0, /device:TPU:1, one launch (start us, length us, event | category | flops | bytes accessed | tf_op | source)
XLA Modules:
  0.0 465.2 jit_solution(2830314117835366311)
XLA Ops:
  8.5 2.6 collective-permute-start
  11.1 7.9 %collective-permute-start.1 = (bf16[128,2048]{1,0:T(8,128)(2,1)S(1)}, bf16[128,2048]{1,0:T(8,128)(2,1)S(1)}, u32[]{:S(2)}, u32[]{:S(2)}) collective-permute-start(bf16[128,2048]{1,0:T(8,128)(2,1)S(1)} %get-tuple-element.251), channel_id=1, source_target_pairs={{1,0},{2,1},{3,2},{4,3},{5,4},{6,5},{7,6},{0,7},{9,8},{10,9},{11,1... | collective-permute-start | bytes 1572872 | tf_op jit(solution)/shard_map/ppermute | solution.py:19
  20.6 3.2 pad_maximum_fusion.1
  23.8 3.0 broadcast_in_dim.66
  26.8 167.1 %while.19 = (s32[]{:T(128)}, f32[5,128,2048]{2,1,0:T(8,128)}, bf16[2,128,1024]{2,1,0:T(8,128)(2,1)}, bf16[2,128,1024]{2,1,0:T(8,128)(2,1)}, s32[2,4]{1,0:T(2,128...) while((s32[]{:T(128)}, f32[5,128,2048]{2,1,0:T(8,128)}, ...), condition=%wide.region_5.6_spmd.clone, body=%wide.region_0.5_spmd.clone.sunk | while | flops 831007872 | bytes 102807848 | solution.py:113
  26.8 2.4 gather_fusion
  34.4 3.5 fusion.97
  40.8 2.8 fusion.98
  43.6 17.3 %fusion.100 = bf16[16,64,128]{2,1,0:T(8,128)(2,1)S(1)} fusion(bf16[512,16,64]{0,2,1:T(8,128)(2,1)S(1)} %bitcast.107, f32[16,128,512]{2,1,0:T(8,128)} %fusion.98, f32[16,128,512]{2,1,0:T(8,128)} %get-tuple-element.320, f32[16,128]{1,0:T(8,128)S(1)} %get-tuple-element.321), kind=kOutput, calls=%fused_computation.23.clone.1 | convolution fusion | flops 141691392 | bytes 9707520 | tf_op jit(solution)/shard_map/while/body/eval_jaxpr/hqk,khd->qhd/dot_general | solution.py:60
  61.0 3.2 fusion.101
  66.0 18.8 %fusion.99 = f32[512,16,64]{0,2,1:T(8,128)} fusion(bf16[128,16,64]{0,2,1:T(8,128)(2,1)S(1)} %bitcast.110, f32[16,128,512]{2,1,0:T(8,128)} %fusion.98, f32[16,128,512]{2,1,0:T(8,128)} %get-tuple-element.320, f32[16,128]{1,0:T(8,128)S(1)} %get-tuple-element.321), kind=kOutput, calls=%fused_computation.21.clone.1 | convolution fusion | flops 141560320 | bytes 10756096 | tf_op jit(solution)/shard_map/while/body/eval_jaxpr/hqk,qhd->khd/dot_general | solution.py:62
  84.8 1.9 concatenate.25
  88.6 4.1 convolution_bitcast_fusion.2
  94.7 1.9 copy.50
  96.6 4.7 %pad_maximum_fusion.3 = f32[4,128,2048]{2,1,0:T(8,128)} fusion(f32[4,128,1024]{2,1,0:T(8,128)} %copy.50, f32[4,128,1024]{2,1,0:T(8,128)} %copy.52), kind=kLoop, calls=%fused_computation.6.clone.1 | loop fusion | flops 1048576 | bytes 8388608 | tf_op jit(solution)/shard_map/while/body/eval_jaxpr/concatenate | solution.py:65
  101.4 9.0 %scatter_fusion = f32[5,128,2048]{2,1,0:T(8,128)} fusion(f32[5,128,2048]{2,1,0:T(8,128)} %get-tuple-element.337, s32[4]{0:T(128)S(1)} %fusion.94, f32[4,128,2048]{2,1,0:T(8,128)} %pad_maximum_fusion.3), kind=kCustom, calls=%fused_computation.1.clone.clone.1 | custom fusion | flops 1048576 | bytes 12582928 | tf_op jit(solution)/shard_map/while/body/eval_jaxpr/scatter-add | solution.py:100
  110.4 2.4 gather_fusion
  118.0 3.5 fusion.97
  124.4 2.8 fusion.98
  127.2 17.3 %fusion.100 = bf16[16,64,128]{2,1,0:T(8,128)(2,1)S(1)} fusion(bf16[512,16,64]{0,2,1:T(8,128)(2,1)S(1)} %bitcast.107, f32[16,128,512]{2,1,0:T(8,128)} %fusion.98, f32[16,128,512]{2,1,0:T(8,128)} %get-tuple-element.320, f32[16,128]{1,0:T(8,128)S(1)} %get-tuple-element.321), kind=kOutput, calls=%fused_computation.23.clone.1 | convolution fusion | flops 141691392 | bytes 9707520 | tf_op jit(solution)/shard_map/while/body/eval_jaxpr/hqk,khd->qhd/dot_general | solution.py:60
  144.6 3.2 fusion.101
  149.6 18.9 %fusion.99 = f32[512,16,64]{0,2,1:T(8,128)} fusion(bf16[128,16,64]{0,2,1:T(8,128)(2,1)S(1)} %bitcast.110, f32[16,128,512]{2,1,0:T(8,128)} %fusion.98, f32[16,128,512]{2,1,0:T(8,128)} %get-tuple-element.320, f32[16,128]{1,0:T(8,128)S(1)} %get-tuple-element.321), kind=kOutput, calls=%fused_computation.21.clone.1 | convolution fusion | flops 141560320 | bytes 10756096 | tf_op jit(solution)/shard_map/while/body/eval_jaxpr/hqk,qhd->khd/dot_general | solution.py:62
  168.4 1.9 concatenate.25
  172.2 4.1 convolution_bitcast_fusion.2
  176.4 1.9 concatenate.24
  178.3 1.9 copy.50
  180.2 4.7 %pad_maximum_fusion.3 = f32[4,128,2048]{2,1,0:T(8,128)} fusion(f32[4,128,1024]{2,1,0:T(8,128)} %copy.50, f32[4,128,1024]{2,1,0:T(8,128)} %copy.52), kind=kLoop, calls=%fused_computation.6.clone.1 | loop fusion | flops 1048576 | bytes 8388608 | tf_op jit(solution)/shard_map/while/body/eval_jaxpr/concatenate | solution.py:65
  185.0 8.9 %scatter_fusion = f32[5,128,2048]{2,1,0:T(8,128)} fusion(f32[5,128,2048]{2,1,0:T(8,128)} %get-tuple-element.337, s32[4]{0:T(128)S(1)} %fusion.94, f32[4,128,2048]{2,1,0:T(8,128)} %pad_maximum_fusion.3), kind=kCustom, calls=%fused_computation.1.clone.clone.1 | custom fusion | flops 1048576 | bytes 12582928 | tf_op jit(solution)/shard_map/while/body/eval_jaxpr/scatter-add | solution.py:100
  195.2 7.9 %collective-permute-start.3 = (f32[128,2048]{1,0:T(8,128)S(1)}, f32[128,2048]{1,0:T(8,128)S(1)}, u32[]{:S(2)}, u32[]{:S(2)}) collective-permute-start(f32[128,2048]{1,0:T(8,128)S(1)} %slice_bitcast_fusion), channel_id=1, source_target_pairs={{1,0},{2,1},{3,2},{4,3},{5,4},{6,5},{7,6},{0,7},{9,8},{10,9},{11,1... | collective-permute-start | bytes 3145736 | tf_op jit(solution)/shard_map/ppermute | solution.py:27
  204.4 2.1 slice.85
  206.5 4.0 collective-permute-done.2
  215.9 241.0 %all-reduce.3.cloned.1.call-done = f32[384,2048]{1,0:T(8,128)} async-done(((f32[384,2048]{1,0:T(8,128)}), f32[384,2048]{1,0:T(8,128)}) %all-reduce.3.cloned.1.call-update) | async-done | bytes 3145744
  (67 shorter events, 37.1 us)
Async XLA Ops:
  7.2 449.7 %all-reduce.3.cloned.1.call-start = ((), (), s32[]{:S(2)}) async-start(), calls=%async_computation | async-start | bytes 6291456
  8.5 11.9 %collective-permute-start = (bf16[128,2048]{1,0:T(8,128)(2,1)S(1)}, bf16[128,2048]{1,0:T(8,128)(2,1)S(1)}, u32[]{:S(2)}, u32[]{:S(2)}) collective-permute-start(bf16[128,2048]{1,0:T(8,128)(2,1)S(1)} %get-tuple-element.250), channel_id=1, source_target_pairs={{0,1},{1,2},{2,3},{3,4},{4,5},{5,6},{6,7},{7,0},{8,9},{9,10},{10,1... | collective-permute-start | bytes 1572872 | tf_op jit(solution)/shard_map/ppermute | solution.py:18
  11.1 9.5 %collective-permute-start.1 = (bf16[128,2048]{1,0:T(8,128)(2,1)S(1)}, bf16[128,2048]{1,0:T(8,128)(2,1)S(1)}, u32[]{:S(2)}, u32[]{:S(2)}) collective-permute-start(bf16[128,2048]{1,0:T(8,128)(2,1)S(1)} %get-tuple-element.251), channel_id=1, source_target_pairs={{1,0},{2,1},{3,2},{4,3},{5,4},{6,5},{7,6},{0,7},{9,8},{10,9},{11,1... | collective-permute-start | bytes 1572872 | tf_op jit(solution)/shard_map/ppermute | solution.py:19
  20.6 6.2 %copy-start.3 = (s32[2]{0:T(128)S(1)}, s32[2]{0:T(128)}, u32[]{:S(2)}) copy-start(s32[2]{0:T(128)} %param.15) | copy-start | bytes 28
  20.6 6.2 %copy-start.4 = (s32[2]{0:T(128)S(1)}, s32[2]{0:T(128)}, u32[]{:S(2)}) copy-start(s32[2]{0:T(128)} %param.16) | copy-start | bytes 28
  61.0 3.4 copy-start.1
  65.2 0.8 copy-start.2
  144.6 3.4 copy-start.1
  148.8 0.8 copy-start.2
  195.2 16.7 %collective-permute-start.3 = (f32[128,2048]{1,0:T(8,128)S(1)}, f32[128,2048]{1,0:T(8,128)S(1)}, u32[]{:S(2)}, u32[]{:S(2)}) collective-permute-start(f32[128,2048]{1,0:T(8,128)S(1)} %slice_bitcast_fusion), channel_id=1, source_target_pairs={{1,0},{2,1},{3,2},{4,3},{5,4},{6,5},{7,6},{0,7},{9,8},{10,9},{11,1... | collective-permute-start | bytes 3145736 | tf_op jit(solution)/shard_map/ppermute | solution.py:27
  204.4 6.1 %collective-permute-start.2 = (bf16[128,2048]{1,0:T(8,128)(2,1)S(1)}, bf16[128,2048]{1,0:T(8,128)(2,1)S(1)}, u32[]{:S(2)}, u32[]{:S(2)}) collective-permute-start(bf16[128,2048]{1,0:T(8,128)(2,1)S(1)} %fusion.52), channel_id=1, source_target_pairs={{7,0},{0,1},{1,2},{2,3},{3,4},{4,5},{5,6},{6,7},{15,8},{8,9},{9,10... | collective-permute-start | bytes 1572872 | tf_op jit(solution)/shard_map/ppermute | solution.py:27
  212.2 1.7 copy-start
Sparse Core Ops, SparseCore 0:
  214.0 242.7 all-reduce.2
where the time goes:
time: 472 us; the launch traced here: 465 us
  waiting for transfers between devices  246 us (52%)
  matrix products  99.4 us (21%)
  local copies, waits for them, and re-layouts  50.7 us (11%)
  other arithmetic  35.6 us (8%)
  starting transfers between devices  18.5 us (4%)
  between operations  14.8 us (3%)
    unnamed x2, waiting for transfers between devices  241 us
    dot_general x2, matrix products, block_pass(): jnp.einsum('hqk,qhd->khd', grad_low, query_heads, preferred_element_type=...  37.7 us
    dot_general x2, matrix products, block_pass(): jnp.einsum('hqk,khd->qhd', grad_low, key_heads, preferred_element_type=jn...  34.5 us
    scatter-add x2, other arithmetic, advance(): grad_window.at[slot_ids]  17.9 us
    concatenate x8, local copies, waits for them, and re-layouts, block_pass(): jnp.concatenate([grad_keys.reshape(kv_rows.shape[0], feature_count), grad...  15.3 us
    concatenate x2, other arithmetic, block_pass(): jnp.concatenate([grad_keys.reshape(kv_rows.shape[0], feature_count), grad...  9.46 us
  transfers between devices with their start and end apart: 5, of which 4 were waited for; matrix products, arithmetic and copies ran while one was open for 1% of the time, Pallas kernels for 0%

commit v1 on v0

v1 whole, which is shorter than its diff:
```python
import functools
import math

import jax
import jax.numpy as jnp
from jax import lax
from jax.experimental import pallas as pl
from jax.experimental.pallas import tpu as pltpu
from jax.sharding import PartitionSpec as P

H = 16
HEAD = 64
NY, NZ = 8, 12
BLOCK = 128
WIN = 5
QUADS = 4
HEADS = H // QUADS
QUAD = HEADS * HEAD
MESH = pl.DeviceIdType.MESH
SCALE = 1.0 / math.sqrt(HEAD)
LOG2E = 1.4426950408889634
F32, BF16 = jnp.float32, jnp.bfloat16
FIRST_AXIS = ("y", "z", "y", "y")


def dot(a, b):
    return jnp.dot(a, b, preferred_element_type=F32)


def slot_bias(blocks_ref, count_ref, region, n, w, total):
    wanted = lax.rem(3 * region - 1 + w + total, total)
    uses = 0
    for p in range(blocks_ref.shape[1]):
        live = (blocks_ref[n, p] == wanted) & (p < count_ref[n])
        uses = uses + jnp.where(live, 1, 0)
    return jnp.where(
        uses == 0,
        F32(-1e30),
        jnp.where(
            uses == 1,
            F32(0.0),
            jnp.where(uses == 2, F32(1.0), jnp.where(uses == 3, F32(math.log2(3.0)), F32(2.0))),
        ),
    )


def owner_tiles(keys, values):
    rows = keys.shape[0]
    low = lax.broadcasted_iota(jnp.int32, (rows // 8, 8, 128), 1) < 4

    def split(a, lane):
        return a[:, lane : lane + 128].reshape(rows // 8, 8, 128)

    def pair(a):
        left, right = split(a, 0), split(a, 128)
        even = jnp.where(low, left, pltpu.roll(right, 4, 1))
        odd = jnp.where(low, pltpu.roll(left, 4, 1), right)
        return even, odd

    key_even, key_odd = pair(keys)
    value_even, value_odd = pair(values)
    even = jnp.concatenate([key_even, value_even], axis=1)
    odd = jnp.concatenate([key_odd, value_odd], axis=1)
    return jnp.stack([even, odd], axis=1).reshape(rows // 4, 16, 128)


def kernel(
    queries, latent, blocks, pair_count, obs_count, cotangent,
    attended, grad_query, grad_kv,
    window, middle, rim_out, rim_in, part, first_in, second_out, second_in,
    local_sem, halo_send, halo_recv, rim_send, rim_recv,
    first_send, first_recv, second_send, second_recv,
):
    place, region = lax.axis_index("obs"), lax.axis_index("grid")
    regions = lax.axis_size("grid")
    y, z = place // NZ, lax.rem(place, NZ)
    after = (place, lax.rem(region + 1, regions))
    before = (place, lax.rem(region + regions - 1, regions))

    def along(axis, k):
        if axis == "y":
            return lax.rem(y + k, NY)
        return lax.rem(z + k, NZ)

    def peer(axis, k):
        if axis == "y":
            return (along(axis, k) * NZ + z, region)
        return (y * NZ + along(axis, k), region)

    peers = [peer("y", k) for k in range(1, NY)] + [peer("z", k) for k in range(1, NZ)]
    barrier = pltpu.get_barrier_semaphore()
    for device in [after, before] + peers:
        pl.semaphore_signal(barrier, inc=1, device_id=device, device_id_type=MESH)

    own = pltpu.make_async_copy(latent.at[0], window.at[pl.ds(BLOCK, 3 * BLOCK)], local_sem)
    own.start()
    pl.semaphore_wait(barrier, 2 + len(peers))

    def halo_copies(g):
        copies = []
        for part_at in range(2):
            columns = pl.ds(part_at * H * HEAD + g * QUAD, QUAD)
            for side, device in enumerate((after, before)):
                source = 2 * BLOCK if side == 0 else 0
                target = 0 if side == 0 else 4 * BLOCK
                copies.append(
                    pltpu.make_async_remote_copy(
                        src_ref=latent.at[0, pl.ds(source, BLOCK), columns],
                        dst_ref=window.at[pl.ds(target, BLOCK), columns],
                        send_sem=halo_send.at[g, part_at, side],
                        recv_sem=halo_recv.at[g, part_at, side],
                        device_id=device,
                        device_id_type=MESH,
                    )
                )
        return copies

    halos = [halo_copies(g) for g in range(QUADS)]
    for copies in halos:
        for copy in copies:
            copy.start()

    lane = lax.broadcasted_iota(jnp.int32, (1, 2 * BLOCK), 1)
    in_first = lane < BLOCK
    bias = [
        jnp.where(
            in_first,
            slot_bias(blocks, pair_count, region, 0, w, 3 * regions),
            slot_bias(blocks, pair_count, region, 1, w, 3 * regions),
        )
        for w in range(WIN)
    ]
    lane_live = lane < jnp.where(in_first, obs_count[0], BLOCK + obs_count[1])
    row = lax.broadcasted_iota(jnp.int32, (2 * BLOCK, 1), 0)
    row_live = row < jnp.where(row < BLOCK, obs_count[0], BLOCK + obs_count[1])
    head_lane = lax.broadcasted_iota(jnp.int32, (2 * BLOCK, QUAD), 1) // HEAD

    def compute(g):
        columns = pl.ds(g * QUAD, QUAD)
        value_columns = pl.ds(H * HEAD + g * QUAD, QUAD)
        query = queries[:, columns]
        grad = jnp.where(row_live, cotangent[:, columns], 0).astype(BF16)
        query_t, grad_t = query.T, grad.T
        keys, values = window[:, columns], window[:, value_columns]
        keys_t, values_t = keys.T, values.T
        mixed, query_grads = [], []
        key_grads = value_grads = None
        for h in range(HEADS):
            rows = slice(h * HEAD, (h + 1) * HEAD)

            def alone(a):
                pieces = []
                if h > 0:
                    pieces.append(jnp.zeros((h * HEAD, a.shape[1]), a.dtype))
                pieces.append(a[rows])
                if h < HEADS - 1:
                    pieces.append(jnp.zeros(((HEADS - 1 - h) * HEAD, a.shape[1]), a.dtype))
                return jnp.concatenate(pieces, axis=0)

            scores = dot(keys, alone(query_t))
            tops = [
                jnp.max(scores[w * BLOCK : (w + 1) * BLOCK], axis=0, keepdims=True) * (SCALE * LOG2E) + bias[w]
                for w in range(WIN)
            ]
            top = functools.reduce(jnp.maximum, tops)
            shift = jnp.concatenate(
                [jnp.broadcast_to(top - bias[w], (BLOCK, 2 * BLOCK)) for w in range(WIN)], axis=0
            )
            expanded = jnp.exp2(scores * (SCALE * LOG2E) - shift)
            attention = expanded * (1.0 / jnp.sum(expanded, axis=0, keepdims=True))
            attention_low = attention.astype(BF16)
            grad_attention = dot(values, alone(grad_t))
            delta = jnp.sum(attention * grad_attention, axis=0, keepdims=True)
            grad_low = (attention * ((grad_attention - delta) * SCALE)).astype(BF16)
            mixed.append(dot(values_t[rows], attention_low))
            query_grads.append(dot(keys_t[rows], grad_low))
            mine = head_lane == h
            key_part = dot(grad_low, jnp.where(mine, query, 0).astype(BF16))
            value_part = dot(attention_low, jnp.where(mine, grad, 0).astype(BF16))
            key_grads = key_part if key_grads is None else key_grads + key_part
            value_grads = value_part if value_grads is None else value_grads + value_part
        mixed = jnp.where(lane_live, jnp.concatenate(mixed, axis=0), 0.0)
        attended[:, columns] = mixed.T.astype(BF16)
        grad_query[:, columns] = jnp.concatenate(query_grads, axis=0).T.astype(BF16)
        tiles = owner_tiles(key_grads, value_grads)
        rim_out[g, 0] = tiles[:32].astype(BF16)
        middle[g] = tiles[32:128]
        rim_out[g, 1] = tiles[128:].astype(BF16)

    def rim_copies(g):
        return [
            pltpu.make_async_remote_copy(
                src_ref=rim_out.at[g, side],
                dst_ref=rim_in.at[g, side],
                send_sem=rim_send.at[g, side],
                recv_sem=rim_recv.at[g, side],
                device_id=device,
                device_id_type=MESH,
            )
            for side, device in enumerate((before, after))
        ]

    def exchange(axis, source, target, send, recv):
        copies = []
        for k in range(1, NY if axis == "y" else NZ):
            copies.append(
                pltpu.make_async_remote_copy(
                    src_ref=source(along(axis, k)),
                    dst_ref=target(k - 1),
                    send_sem=send(k - 1),
                    recv_sem=recv(k - 1),
                    device_id=peer(axis, k),
                    device_id_type=MESH,
                )
            )
        return copies

    def piece(g, axis, i):
        return part.at[g, i] if axis == "y" else part.at[g, :, i]

    def landing(g, axis, k):
        if axis == "y":
            return first_in.at[g, k, pl.ds(0, NZ)]
        return first_in.at[g, k, pl.ds(0, NY)]

    def first_copies(g):
        axis = FIRST_AXIS[g]
        return exchange(
            axis,
            lambda i: piece(g, axis, i),
            lambda k: landing(g, axis, k),
            lambda k: first_send.at[g, k],
            lambda k: first_recv.at[g, k],
        )

    def second_copies(g):
        axis = "z" if FIRST_AXIS[g] == "y" else "y"
        return exchange(
            axis,
            lambda i: second_out.at[g, i],
            lambda k: second_in.at[g, k],
            lambda k: second_send.at[g, k],
            lambda k: second_recv.at[g, k],
        )

    def start_first(g, rims):
        for copy in rims:
            copy.wait_recv()
        half = part.at[g]
        for i in range(NY):
            owned = middle[g, i * NZ : (i + 1) * NZ]
            for side, start in ((1, 0), (0, 64)):
                low, high = max(i * NZ, start), min((i + 1) * NZ, start + 32)
                if low < high:
                    extra = rim_in[g, side, low - start : high - start].astype(F32)
                    pieces = [extra]
                    if low > i * NZ:
                        pieces.insert(0, jnp.zeros((low - i * NZ, 16, 128), F32))
                    if high < (i + 1) * NZ:
                        pieces.append(jnp.zeros(((i + 1) * NZ - high, 16, 128), F32))
                    owned = owned + jnp.concatenate(pieces, axis=0)
            half[i] = owned.astype(BF16)
        copies = first_copies(g)
        for copy in copies:
            copy.start()
        return copies

    def start_second(g, copies):
        for copy in copies:
            copy.wait_recv()
        axis = FIRST_AXIS[g]
        mine = along(axis, 0)
        total = piece(g, axis, mine)[...].astype(F32)
        for k in range(len(copies)):
            total = total + landing(g, axis, k)[...].astype(F32)
        count = total.shape[0]
        second_out[g, 0:count] = total.astype(BF16)
        copies = second_copies(g)
        for copy in copies:
            copy.start()
        return copies

    def finish(g, copies):
        for copy in copies:
            copy.wait_recv()
        axis = "z" if FIRST_AXIS[g] == "y" else "y"
        total = second_out[g, along(axis, 0)].astype(F32)
        for k in range(len(copies)):
            total = total + second_in[g, k].astype(F32)
        for c in range(4):
            start = (c // 2) * H * HEAD + g * QUAD + (c % 2) * 128
            grad_kv[0, :, start : start + 128] = total[4 * c : 4 * c + 4]

    own.wait()
    rims, firsts, seconds = {}, {}, {}
    for g in range(QUADS):
        for copy in halos[g]:
            copy.wait_recv()
        compute(g)
        rims[g] = rim_copies(g)
        for copy in rims[g]:
            copy.start()
        if g >= 1:
            firsts[g - 1] = start_first(g - 1, rims[g - 1])
        if g >= 2:
            seconds[g - 2] = start_second(g - 2, firsts[g - 2])
    last = QUADS - 1
    firsts[last] = start_first(last, rims[last])
    seconds[last - 1] = start_second(last - 1, firsts[last - 1])
    seconds[last] = start_second(last, firsts[last])
    for g in range(QUADS):
        finish(g, seconds[g])
    for groups in (halos, rims.values(), firsts.values(), seconds.values()):
        for copies in groups:
            for copy in copies:
                copy.wait_send()


def per_device(queries, latent_kv, pair_blocks, pair_count, obs_count, cotangent):
    vmem = pl.BlockSpec(memory_space=pltpu.VMEM)
    smem = pl.BlockSpec(memory_space=pltpu.SMEM)
    hbm = pl.BlockSpec(memory_space=pl.ANY)
    rows, width = queries.shape
    dma = pltpu.SemaphoreType.DMA
    return pl.pallas_call(
        kernel,
        out_shape=(
            jax.ShapeDtypeStruct((rows, width), BF16),
            jax.ShapeDtypeStruct((rows, width), BF16),
            jax.ShapeDtypeStruct((1, 4, 2 * width), F32),
        ),
        in_specs=[vmem, hbm, smem, smem, smem, vmem],
        out_specs=(vmem, vmem, vmem),
        scratch_shapes=[
            pltpu.VMEM((WIN * BLOCK, 2 * width), BF16),
            pltpu.VMEM((QUADS, NY * NZ, 16, 128), F32),
            pltpu.VMEM((QUADS, 2, 32, 16, 128), BF16),
            pltpu.VMEM((QUADS, 2, 32, 16, 128), BF16),
            pltpu.VMEM((QUADS, NY, NZ, 16, 128), BF16),
            pltpu.VMEM((QUADS, NZ - 1, NZ, 16, 128), BF16),
            pltpu.VMEM((QUADS, NZ, 16, 128), BF16),
            pltpu.VMEM((QUADS, NZ - 1, 16, 128), BF16),
            dma,
            dma((QUADS, 2, 2)),
            dma((QUADS, 2, 2)),
            dma((QUADS, 2)),
            dma((QUADS, 2)),
            dma((QUADS, NZ - 1)),
            dma((QUADS, NZ - 1)),
            dma((QUADS, NZ - 1)),
            dma((QUADS, NZ - 1)),
        ],
        compiler_params=pltpu.CompilerParams(
            collective_id=0, has_side_effects=True, vmem_limit_bytes=56 * 1024 * 1024
        ),
    )(queries, latent_kv, pair_blocks, pair_count, obs_count, cotangent)


def solution(mesh):
    placed = (
        P(("obs", "grid"), None),
        P("grid", None, None),
        P(("obs", "grid"), None),
        P(("obs", "grid")),
        P(("obs", "grid")),
        P(("obs", "grid"), None),
    )
    return jax.shard_map(
        per_device,
        mesh=mesh,
        in_specs=placed,
        out_specs=(P(("obs", "grid"), None), P(("obs", "grid"), None), P("grid", "obs", None)),
        check_vma=False,
    )
```

time: 472 us -> 82.7 us (0.18)
  the two profiles are of different devices: /device:TPU:1 before, /device:TPU:2 now
where the time goes in v1:
time: 82.7 us; the launch traced here: 82.5 us
  Pallas kernels  77.5 us (94%)
  local copies, waits for them, and re-layouts  4.36 us (5%)
    pallas_call x1, Pallas kernels, per_device(): pl.pallas_call(kernel, out_shape=(jax.ShapeDtypeStruct((rows, width), BF1...  77.5 us
    unnamed x5, local copies, waits for them, and re-layouts  4.36 us

profile of v1, /device:TPU:2, one launch (start us, length us, event | category | flops | bytes accessed | tf_op | source)
XLA Modules:
  0.0 82.5 jit_solution(11818925247074433549)
XLA Ops:
  0.6 77.5 %shard_map.85 = (bf16[256,1024]{1,0:T(8,128)(2,1)}, bf16[256,1024]{1,0:T(8,128)(2,1)}, f32[1,4,2048]{2,1,0:T(4,128)}) custom-call(bf16[256,1024]{1,0:T(8,128)(2,1)} %queries.1, bf16[1,384,2048]{2,1,0:T(8,128)(2,1)} %latent.1, s32[2,4]{1,0:T(2,128)} %blocks.1, s32[2]{0:T(128)} %pair_count.1, s32[2]{0:T(128)} %obs_count.1, bf16[256,1024]{1,0:T(8,128)(2,1)} %cotangent.1), custom_call_target="tpu_custom_call" | custom-call | tf_op jit(solution)/shard_map/pallas_call | solution.py:325
  78.1 0.0 copy-start
  78.1 1.9 %copy.12 = bf16[256,1024]{1,0:T(8,128)(2,1)} copy(bf16[256,1024]{1,0:T(8,128)(2,1)} %get-tuple-element.6) | data formatting | bytes 1048576
  80.0 1.9 %copy.13 = bf16[256,1024]{1,0:T(8,128)(2,1)} copy(bf16[256,1024]{1,0:T(8,128)(2,1)} %get-tuple-element.7) | data formatting | bytes 1048576
  81.9 0.0 copy-done
  81.9 0.6 copy.14
Async XLA Ops:
  78.1 3.8 %copy-start = (f32[1,4,2048]{2,1,0:T(4,128)S(1)}, f32[1,4,2048]{2,1,0:T(4,128)}, u32[]{:S(2)}) copy-start(f32[1,4,2048]{2,1,0:T(4,128)} %get-tuple-element.8) | copy-start | bytes 98308

commit v2 on v1

--- a/solution.py
+++ b/solution.py
@@ -20,7 +20,11 @@
 SCALE = 1.0 / math.sqrt(HEAD)
 LOG2E = 1.4426950408889634
 F32, BF16 = jnp.float32, jnp.bfloat16
-FIRST_AXIS = ("y", "z", "y", "y")
+FIRST_AXIS = ("z", "y", "y", "y")
+RUNS = {
+    "y": ((1, 4, 3), (1, 2, 1), (-1, 3, 2), (-1, 1, 1)),
+    "z": ((1, 6, 5), (1, 4, 3), (1, 2, 1), (-1, 5, 4), (-1, 3, 2), (-1, 1, 1)),
+}
 
 
 def dot(a, b):
@@ -67,7 +71,7 @@
 def kernel(
     queries, latent, blocks, pair_count, obs_count, cotangent,
     attended, grad_query, grad_kv,
-    window, middle, rim_out, rim_in, part, first_in, second_out, second_in,
+    query_in, grad_in, lows, grad_lows, window, middle, rim_out, rim_in, part, first_in, hop_out, second_out, second_in,
     local_sem, halo_send, halo_recv, rim_send, rim_recv,
     first_send, first_recv, second_send, second_recv,
 ):
@@ -79,8 +83,8 @@
 
     def along(axis, k):
         if axis == "y":
-            return lax.rem(y + k, NY)
-        return lax.rem(z + k, NZ)
+            return lax.rem(y + k + NY, NY)
+        return lax.rem(z + k + NZ, NZ)
 
     def peer(axis, k):
         if axis == "y":
@@ -92,8 +96,13 @@
     for device in [after, before] + peers:
         pl.semaphore_signal(barrier, inc=1, device_id=device, device_id_type=MESH)
 
-    own = pltpu.make_async_copy(latent.at[0], window.at[pl.ds(BLOCK, 3 * BLOCK)], local_sem)
-    own.start()
+    loads = [
+        pltpu.make_async_copy(latent.at[0], window.at[pl.ds(BLOCK, 3 * BLOCK)], local_sem.at[0]),
+        pltpu.make_async_copy(queries, query_in, local_sem.at[1]),
+        pltpu.make_async_copy(cotangent, grad_in, local_sem.at[2]),
+    ]
+    for copy in loads:
+        copy.start()
     pl.semaphore_wait(barrier, 2 + len(peers))
 
     def halo_copies(g):
@@ -138,26 +147,28 @@
     def compute(g):
         columns = pl.ds(g * QUAD, QUAD)
         value_columns = pl.ds(H * HEAD + g * QUAD, QUAD)
-        query = queries[:, columns]
-        grad = jnp.where(row_live, cotangent[:, columns], 0).astype(BF16)
+        query = query_in[:, columns]
+        grad = jnp.where(row_live, grad_in[:, columns], 0).astype(BF16)
         query_t, grad_t = query.T, grad.T
         keys, values = window[:, columns], window[:, value_columns]
-        keys_t, values_t = keys.T, values.T
-        mixed, query_grads = [], []
-        key_grads = value_grads = None
+        def alone(a, h):
+            rows = slice(h * HEAD, (h + 1) * HEAD)
+            pieces = []
+            if h > 0:
+                pieces.append(jnp.zeros((h * HEAD, a.shape[1]), a.dtype))
+            pieces.append(a[rows])
+            if h < HEADS - 1:
+                pieces.append(jnp.zeros(((HEADS - 1 - h) * HEAD, a.shape[1]), a.dtype))
+            return jnp.concatenate(pieces, axis=0)
+
+        def front(h):
+            return dot(keys, alone(query_t, h)), dot(values, alone(grad_t, h))
+
+        ready = front(0)
         for h in range(HEADS):
-            rows = slice(h * HEAD, (h + 1) * HEAD)
-
-            def alone(a):
-                pieces = []
-                if h > 0:
-                    pieces.append(jnp.zeros((h * HEAD, a.shape[1]), a.dtype))
-                pieces.append(a[rows])
-                if h < HEADS - 1:
-                    pieces.append(jnp.zeros(((HEADS - 1 - h) * HEAD, a.shape[1]), a.dtype))
-                return jnp.concatenate(pieces, axis=0)
-
-            scores = dot(keys, alone(query_t))
+            scores, grad_attention = ready
+            if h < HEADS - 1:
+                ready = front(h + 1)
             tops = [
                 jnp.max(scores[w * BLOCK : (w + 1) * BLOCK], axis=0, keepdims=True) * (SCALE * LOG2E) + bias[w]
                 for w in range(WIN)
@@ -169,23 +180,43 @@
             expanded = jnp.exp2(scores * (SCALE * LOG2E) - shift)
             attention = expanded * (1.0 / jnp.sum(expanded, axis=0, keepdims=True))
             attention_low = attention.astype(BF16)
-            grad_attention = dot(values, alone(grad_t))
             delta = jnp.sum(attention * grad_attention, axis=0, keepdims=True)
             grad_low = (attention * ((grad_attention - delta) * SCALE)).astype(BF16)
-            mixed.append(dot(values_t[rows], attention_low))
-            query_grads.append(dot(keys_t[rows], grad_low))
-            mine = head_lane == h
-            key_part = dot(grad_low, jnp.where(mine, query, 0).astype(BF16))
-            value_part = dot(attention_low, jnp.where(mine, grad, 0).astype(BF16))
-            key_grads = key_part if key_grads is None else key_grads + key_part
-            value_grads = value_part if value_grads is None else value_grads + value_part
+            lows[g * HEADS + h] = attention_low
+            grad_lows[g * HEADS + h] = grad_low
+
+        def spread(a):
+            return jnp.concatenate([jnp.where(head_lane == h, a, 0).astype(BF16) for h in range(HEADS)], axis=0)
+
+        query_spread, grad_spread = spread(query), spread(grad)
+
+        def grad_tiles(start, count):
+            at = slice(start * BLOCK, (start + count) * BLOCK)
+
+            def heads(ref):
+                return jnp.concatenate([ref[g * HEADS + h, at] for h in range(HEADS)], axis=1)
+
+            return owner_tiles(dot(heads(grad_lows), query_spread), dot(heads(lows), grad_spread))
+
+        rim_out[g, 0] = grad_tiles(0, 1).astype(BF16)
+        rim_out[g, 1] = grad_tiles(4, 1).astype(BF16)
+        rims[g] = rim_copies(g)
+        for copy in rims[g]:
+            copy.start()
+        middle[g] = grad_tiles(1, 3)
+
+    def hand_over(g):
+        columns = pl.ds(g * QUAD, QUAD)
+        keys_t = window[:, columns].T
+        values_t = window[:, pl.ds(H * HEAD + g * QUAD, QUAD)].T
+        mixed, query_grads = [], []
+        for h in range(HEADS):
+            rows = slice(h * HEAD, (h + 1) * HEAD)
+            mixed.append(dot(values_t[rows], lows[g * HEADS + h]))
+            query_grads.append(dot(keys_t[rows], grad_lows[g * HEADS + h]))
         mixed = jnp.where(lane_live, jnp.concatenate(mixed, axis=0), 0.0)
         attended[:, columns] = mixed.T.astype(BF16)
         grad_query[:, columns] = jnp.concatenate(query_grads, axis=0).T.astype(BF16)
-        tiles = owner_tiles(key_grads, value_grads)
-        rim_out[g, 0] = tiles[:32].astype(BF16)
-        middle[g] = tiles[32:128]
-        rim_out[g, 1] = tiles[128:].astype(BF16)
 
     def rim_copies(g):
         return [
@@ -202,7 +233,8 @@
 
     def exchange(axis, source, target, send, recv):
         copies = []
-        for k in range(1, NY if axis == "y" else NZ):
+        size = NY if axis == "y" else NZ
+        for k in sorted(range(1, size), key=lambda k: -min(k, size - k)):
             copies.append(
                 pltpu.make_async_remote_copy(
                     src_ref=source(along(axis, k)),
@@ -223,15 +255,21 @@
             return first_in.at[g, k, pl.ds(0, NZ)]
         return first_in.at[g, k, pl.ds(0, NY)]
 
-    def first_copies(g):
-        axis = FIRST_AXIS[g]
-        return exchange(
-            axis,
-            lambda i: piece(g, axis, i),
-            lambda k: landing(g, axis, k),
-            lambda k: first_send.at[g, k],
-            lambda k: first_recv.at[g, k],
+    def first_copy(g, axis, source, k, slot):
+        return pltpu.make_async_remote_copy(
+            src_ref=source,
+            dst_ref=landing(g, axis, slot),
+            send_sem=first_send.at[g, slot],
+            recv_sem=first_recv.at[g, slot],
+            device_id=peer(axis, k),
+            device_id_type=MESH,
         )
+
+    def runs_of(g):
+        axis, turn = FIRST_AXIS[g], 1 if g % 2 else -1
+        runs = [(turn * sign, far, near) for sign, far, near in RUNS[axis]]
+        pairs = [run for run in runs if run[1] != run[2]]
+        return axis, pairs, [run for run in runs if run[1] == run[2]]
 
     def second_copies(g):
         axis = "z" if FIRST_AXIS[g] == "y" else "y"
@@ -260,19 +298,41 @@
                         pieces.append(jnp.zeros(((i + 1) * NZ - high, 16, 128), F32))
                     owned = owned + jnp.concatenate(pieces, axis=0)
             half[i] = owned.astype(BF16)
-        copies = first_copies(g)
+        axis, pairs, singles = runs_of(g)
+        copies = []
+        for slot, (sign, far, _) in enumerate(pairs):
+            copies.append(first_copy(g, axis, piece(g, axis, along(axis, sign * far)), sign, slot))
+        for slot, (sign, near, _) in enumerate(singles):
+            at = sign * near
+            slot += 2 * len(pairs)
+            copies.append(first_copy(g, axis, piece(g, axis, along(axis, at)), at, slot))
         for copy in copies:
             copy.start()
         return copies
 
+    def pass_on(g, copies):
+        axis, pairs, _ = runs_of(g)
+        count = NZ if axis == "y" else NY
+        sent = []
+        for slot, (sign, _, near) in enumerate(pairs):
+            copies[slot].wait_recv()
+            own_term = piece(g, axis, along(axis, sign * near))[...].astype(F32)
+            total = own_term + landing(g, axis, slot)[...].astype(F32)
+            staged = hop_out.at[g, slot, pl.ds(0, count)]
+            staged[...] = total.astype(BF16)
+            copy = first_copy(g, axis, staged, sign * near, len(pairs) + slot)
+            copy.start()
+            sent.append(copy)
+        return sent + copies[len(pairs) :], copies[: len(pairs)]
+
     def start_second(g, copies):
         for copy in copies:
             copy.wait_recv()
-        axis = FIRST_AXIS[g]
+        axis, pairs, _ = runs_of(g)
         mine = along(axis, 0)
         total = piece(g, axis, mine)[...].astype(F32)
         for k in range(len(copies)):
-            total = total + landing(g, axis, k)[...].astype(F32)
+            total = total + landing(g, axis, len(pairs) + k)[...].astype(F32)
         count = total.shape[0]
         second_out[g, 0:count] = total.astype(BF16)
         copies = second_copies(g)
@@ -291,29 +351,43 @@
             start = (c // 2) * H * HEAD + g * QUAD + (c % 2) * 128
             grad_kv[0, :, start : start + 128] = total[4 * c : 4 * c + 4]
 
-    own.wait()
-    rims, firsts, seconds = {}, {}, {}
-    for g in range(QUADS):
+    for copy in loads:
+        copy.wait()
+    rims, firsts, finals, passed, seconds = {}, {}, {}, {}, {}
+
+    def front(g):
         for copy in halos[g]:
             copy.wait_recv()
         compute(g)
-        rims[g] = rim_copies(g)
-        for copy in rims[g]:
-            copy.start()
-        if g >= 1:
-            firsts[g - 1] = start_first(g - 1, rims[g - 1])
-        if g >= 2:
-            seconds[g - 2] = start_second(g - 2, firsts[g - 2])
-    last = QUADS - 1
-    firsts[last] = start_first(last, rims[last])
-    seconds[last - 1] = start_second(last - 1, firsts[last - 1])
-    seconds[last] = start_second(last, firsts[last])
+
+    def first(g):
+        firsts[g] = start_first(g, rims[g])
+
+    def passing(g):
+        finals[g], passed[g] = pass_on(g, firsts[g])
+
+    def second(g):
+        seconds[g] = start_second(g, finals[g])
+
+    plan = (
+        (front, 0), (front, 1), (front, 2), (first, 0), (front, 3), (first, 1), (hand_over, 0),
+        (first, 2), (passing, 0), (hand_over, 1), (first, 3), (passing, 1), (hand_over, 2),
+        (passing, 2), (hand_over, 3), (passing, 3), (second, 0), (second, 1), (second, 2),
+        (second, 3),
+    )
+    for step, g in plan:
+        step(g)
     for g in range(QUADS):
         finish(g, seconds[g])
-    for groups in (halos, rims.values(), firsts.values(), seconds.values()):
+    for groups in (halos, rims.values(), finals.values(), passed.values(), seconds.values()):
         for copies in groups:
             for copy in copies:
                 copy.wait_send()
+
+
+def hand_out(*refs):
+    for source, target in zip(refs[:3], refs[3:], strict=True):
+        target[...] = source[...]
 
 
 def per_device(queries, latent_kv, pair_blocks, pair_count, obs_count, cotangent):
@@ -322,25 +396,30 @@
     hbm = pl.BlockSpec(memory_space=pl.ANY)
     rows, width = queries.shape
     dma = pltpu.SemaphoreType.DMA
-    return pl.pallas_call(
+    results = pl.pallas_call(
         kernel,
         out_shape=(
             jax.ShapeDtypeStruct((rows, width), BF16),
             jax.ShapeDtypeStruct((rows, width), BF16),
             jax.ShapeDtypeStruct((1, 4, 2 * width), F32),
         ),
-        in_specs=[vmem, hbm, smem, smem, smem, vmem],
+        in_specs=[hbm, hbm, smem, smem, smem, hbm],
         out_specs=(vmem, vmem, vmem),
         scratch_shapes=[
+            pltpu.VMEM((rows, width), BF16),
+            pltpu.VMEM((rows, width), BF16),
+            pltpu.VMEM((H, WIN * BLOCK, rows), BF16),
+            pltpu.VMEM((H, WIN * BLOCK, rows), BF16),
             pltpu.VMEM((WIN * BLOCK, 2 * width), BF16),
             pltpu.VMEM((QUADS, NY * NZ, 16, 128), F32),
             pltpu.VMEM((QUADS, 2, 32, 16, 128), BF16),
             pltpu.VMEM((QUADS, 2, 32, 16, 128), BF16),
             pltpu.VMEM((QUADS, NY, NZ, 16, 128), BF16),
             pltpu.VMEM((QUADS, NZ - 1, NZ, 16, 128), BF16),
+            pltpu.VMEM((QUADS, 5, NZ, 16, 128), BF16),
             pltpu.VMEM((QUADS, NZ, 16, 128), BF16),
             pltpu.VMEM((QUADS, NZ - 1, 16, 128), BF16),
-            dma,
+            dma((3,)),
             dma((QUADS, 2, 2)),
             dma((QUADS, 2, 2)),
             dma((QUADS, 2)),
@@ -354,6 +433,12 @@
             collective_id=0, has_side_effects=True, vmem_limit_bytes=56 * 1024 * 1024
         ),
     )(queries, latent_kv, pair_blocks, pair_count, obs_count, cotangent)
+    return pl.pallas_call(
+        hand_out,
+        out_shape=tuple(jax.ShapeDtypeStruct(r.shape, r.dtype) for r in results),
+        in_specs=[vmem] * 3,
+        out_specs=(vmem,) * 3,
+    )(*results)
 
 
 def solution(mesh):

time: 82.7 us -> 64.7 us (0.78)
  the two profiles are of different devices: /device:TPU:2 before, /device:TPU:1 now
where the time goes in v2:
time: 64.7 us; the launch traced here: 64 us
  Pallas kernels  63.3 us (98%)
    pallas_call x1, Pallas kernels, per_device(): pl.pallas_call(kernel, out_shape=(jax.ShapeDtypeStruct((rows, width), BF1...  61.1 us
    pallas_call x1, Pallas kernels, per_device(): pl.pallas_call(hand_out, out_shape=tuple((jax.ShapeDtypeStruct(r.shape, r...  2.2 us

profile of v2, /device:TPU:1, one launch (start us, length us, event | category | flops | bytes accessed | tf_op | source)
XLA Modules:
  0.0 64.0 jit_solution(13658185014658871616)
XLA Ops:
  0.6 61.1 %shard_map.85 = (bf16[256,1024]{1,0:T(8,128)(2,1)}, bf16[256,1024]{1,0:T(8,128)(2,1)}, f32[1,4,2048]{2,1,0:T(4,128)}) custom-call(bf16[256,1024]{1,0:T(8,128)(2,1)} %queries.1, bf16[1,384,2048]{2,1,0:T(8,128)(2,1)} %latent.1, s32[2,4]{1,0:T(2,128)} %blocks.1, s32[2]{0:T(128)} %pair_count.1, s32[2]{0:T(128)} %obs_count.1, bf16[256,1024]{1,0:T(8,128)(2,1)} %cotangent.1), custom_call_target="tpu_custom_call" | custom-call | tf_op jit(solution)/shard_map/pallas_call | solution.py:399
  61.7 2.2 %shard_map.86 = (bf16[256,1024]{1,0:T(8,128)(2,1)}, bf16[256,1024]{1,0:T(8,128)(2,1)}, f32[1,4,2048]{2,1,0:T(4,128)}) custom-call(bf16[256,1024]{1,0:T(8,128)(2,1)} %get-tuple-element.6.refs_0_, bf16[256,1024]{1,0:T(8,128)(2,1)} %get-tuple-element.7.refs_1_, f32[1,4,2048]{2,1,0:T(4,128)} %get-tuple-element.8.refs_2_), custom_call_target="tpu_custom_call" | custom-call | tf_op jit(solution)/shard_map/pallas_call | solution.py:436

commit v3 on v2

--- a/solution.py
+++ b/solution.py
@@ -20,7 +20,8 @@
 SCALE = 1.0 / math.sqrt(HEAD)
 LOG2E = 1.4426950408889634
 F32, BF16 = jnp.float32, jnp.bfloat16
-FIRST_AXIS = ("z", "y", "y", "y")
+HALO_QUADS = ((0, 1), (1, 1), (2, 2))
+FIRST_AXIS = ("z", "y", "z", "y")
 RUNS = {
     "y": ((1, 4, 3), (1, 2, 1), (-1, 3, 2), (-1, 1, 1)),
     "z": ((1, 6, 5), (1, 4, 3), (1, 2, 1), (-1, 5, 4), (-1, 3, 2), (-1, 1, 1)),
@@ -71,8 +72,9 @@
 def kernel(
     queries, latent, blocks, pair_count, obs_count, cotangent,
     attended, grad_query, grad_kv,
-    query_in, grad_in, lows, grad_lows, window, middle, rim_out, rim_in, part, first_in, hop_out, second_out, second_in,
-    local_sem, halo_send, halo_recv, rim_send, rim_recv,
+    query_in, grad_in, mixed_out, query_grad_out, lows, grad_lows, window, middle,
+    rim_out, rim_in, part, first_in, hop_out, second_out, second_in,
+    local_sem, store_sem, halo_send, halo_recv, rim_send, rim_recv,
     first_send, first_recv, second_send, second_recv,
 ):
     place, region = lax.axis_index("obs"), lax.axis_index("grid")
@@ -81,15 +83,20 @@
     after = (place, lax.rem(region + 1, regions))
     before = (place, lax.rem(region + regions - 1, regions))
 
+    def around(at, k, size):
+        moved = at + k % size
+        return jnp.where(moved >= size, moved - size, moved)
+
+    at_y = [around(y, k, NY) for k in range(NY)]
+    at_z = [around(z, k, NZ) for k in range(NZ)]
+    place_y = [i * NZ + z for i in at_y]
+    place_z = [y * NZ + i for i in at_z]
+
     def along(axis, k):
-        if axis == "y":
-            return lax.rem(y + k + NY, NY)
-        return lax.rem(z + k + NZ, NZ)
+        return at_y[k % NY] if axis == "y" else at_z[k % NZ]
 
     def peer(axis, k):
-        if axis == "y":
-            return (along(axis, k) * NZ + z, region)
-        return (y * NZ + along(axis, k), region)
+        return (place_y[k % NY] if axis == "y" else place_z[k % NZ], region)
 
     peers = [peer("y", k) for k in range(1, NY)] + [peer("z", k) for k in range(1, NZ)]
     barrier = pltpu.get_barrier_semaphore()
@@ -107,8 +114,9 @@
 
     def halo_copies(g):
         copies = []
+        first_quad, count = HALO_QUADS[g]
         for part_at in range(2):
-            columns = pl.ds(part_at * H * HEAD + g * QUAD, QUAD)
+            columns = pl.ds(part_at * H * HEAD + first_quad * QUAD, count * QUAD)
             for side, device in enumerate((after, before)):
                 source = 2 * BLOCK if side == 0 else 0
                 target = 0 if side == 0 else 4 * BLOCK
@@ -124,7 +132,7 @@
                 )
         return copies
 
-    halos = [halo_copies(g) for g in range(QUADS)]
+    halos = [halo_copies(g) for g in range(len(HALO_QUADS))]
     for copies in halos:
         for copy in copies:
             copy.start()
@@ -215,8 +223,12 @@
             mixed.append(dot(values_t[rows], lows[g * HEADS + h]))
             query_grads.append(dot(keys_t[rows], grad_lows[g * HEADS + h]))
         mixed = jnp.where(lane_live, jnp.concatenate(mixed, axis=0), 0.0)
-        attended[:, columns] = mixed.T.astype(BF16)
-        grad_query[:, columns] = jnp.concatenate(query_grads, axis=0).T.astype(BF16)
+        mixed_out[:, columns] = mixed.T.astype(BF16)
+        query_grad_out[:, columns] = jnp.concatenate(query_grads, axis=0).T.astype(BF16)
+        for i, (held, result) in enumerate(((mixed_out, attended), (query_grad_out, grad_query))):
+            copy = pltpu.make_async_copy(held.at[:, columns], result.at[:, columns], store_sem.at[g, i])
+            copy.start()
+            stores.append(copy)
 
     def rim_copies(g):
         return [
@@ -266,10 +278,26 @@
         )
 
     def runs_of(g):
-        axis, turn = FIRST_AXIS[g], 1 if g % 2 else -1
-        runs = [(turn * sign, far, near) for sign, far, near in RUNS[axis]]
-        pairs = [run for run in runs if run[1] != run[2]]
-        return axis, pairs, [run for run in runs if run[1] == run[2]]
+        axis, turn = FIRST_AXIS[g], 1 if g < QUADS // 2 else -1
+        runs, at = [], 0
+        hops = sum(far - near for _, far, near in RUNS[axis])
+        for n, (sign, far, near) in enumerate(RUNS[axis]):
+            runs.append((turn * sign, tuple(range(far, near - 1, -1)), at, hops + n))
+            at += far - near
+        return axis, runs, hops
+
+    def send_step(g, step, source_of):
+        axis, runs, _ = runs_of(g)
+        for run, (sign, distances, at, last) in enumerate(runs):
+            if step >= len(distances):
+                continue
+            source = source_of(axis, run, sign * distances[step], at + step - 1)
+            if step == len(distances) - 1:
+                copy = first_copy(g, axis, source, sign * distances[step], last)
+            else:
+                copy = first_copy(g, axis, source, sign, at + step)
+            copy.start()
+            firsts[g][last if step == len(distances) - 1 else at + step] = copy
 
     def second_copies(g):
         axis = "z" if FIRST_AXIS[g] == "y" else "y"
@@ -298,41 +326,26 @@
                         pieces.append(jnp.zeros(((i + 1) * NZ - high, 16, 128), F32))
                     owned = owned + jnp.concatenate(pieces, axis=0)
             half[i] = owned.astype(BF16)
-        axis, pairs, singles = runs_of(g)
-        copies = []
-        for slot, (sign, far, _) in enumerate(pairs):
-            copies.append(first_copy(g, axis, piece(g, axis, along(axis, sign * far)), sign, slot))
-        for slot, (sign, near, _) in enumerate(singles):
-            at = sign * near
-            slot += 2 * len(pairs)
-            copies.append(first_copy(g, axis, piece(g, axis, along(axis, at)), at, slot))
-        for copy in copies:
-            copy.start()
-        return copies
-
-    def pass_on(g, copies):
-        axis, pairs, _ = runs_of(g)
-        count = NZ if axis == "y" else NY
-        sent = []
-        for slot, (sign, _, near) in enumerate(pairs):
-            copies[slot].wait_recv()
-            own_term = piece(g, axis, along(axis, sign * near))[...].astype(F32)
-            total = own_term + landing(g, axis, slot)[...].astype(F32)
-            staged = hop_out.at[g, slot, pl.ds(0, count)]
+        firsts[g] = {}
+        send_step(g, 0, lambda axis, run, at, slot: piece(g, axis, along(axis, at)))
+
+    def pass_on(g, step):
+        def source_of(axis, run, at, slot):
+            firsts[g][slot].wait_recv()
+            total = piece(g, axis, along(axis, at))[...].astype(F32) + landing(g, axis, slot)[...].astype(F32)
+            staged = hop_out.at[g, slot, pl.ds(0, total.shape[0])]
             staged[...] = total.astype(BF16)
-            copy = first_copy(g, axis, staged, sign * near, len(pairs) + slot)
-            copy.start()
-            sent.append(copy)
-        return sent + copies[len(pairs) :], copies[: len(pairs)]
-
-    def start_second(g, copies):
-        for copy in copies:
-            copy.wait_recv()
-        axis, pairs, _ = runs_of(g)
+            return staged
+
+        send_step(g, step, source_of)
+
+    def start_second(g):
+        axis, runs, hops = runs_of(g)
         mine = along(axis, 0)
         total = piece(g, axis, mine)[...].astype(F32)
-        for k in range(len(copies)):
-            total = total + landing(g, axis, len(pairs) + k)[...].astype(F32)
+        for k in range(hops, hops + len(runs)):
+            firsts[g][k].wait_recv()
+            total = total + landing(g, axis, k)[...].astype(F32)
         count = total.shape[0]
         second_out[g, 0:count] = total.astype(BF16)
         copies = second_copies(g)
@@ -353,41 +366,48 @@
 
     for copy in loads:
         copy.wait()
-    rims, firsts, finals, passed, seconds = {}, {}, {}, {}, {}
+    rims, firsts, seconds, stores = {}, {}, {}, []
 
     def front(g):
-        for copy in halos[g]:
-            copy.wait_recv()
+        if g < len(HALO_QUADS):
+            for copy in halos[g]:
+                copy.wait_recv()
         compute(g)
 
     def first(g):
-        firsts[g] = start_first(g, rims[g])
-
-    def passing(g):
-        finals[g], passed[g] = pass_on(g, firsts[g])
+        start_first(g, rims[g])
 
     def second(g):
-        seconds[g] = start_second(g, finals[g])
+        seconds[g] = start_second(g)
 
     plan = (
-        (front, 0), (front, 1), (front, 2), (first, 0), (front, 3), (first, 1), (hand_over, 0),
-        (first, 2), (passing, 0), (hand_over, 1), (first, 3), (passing, 1), (hand_over, 2),
-        (passing, 2), (hand_over, 3), (passing, 3), (second, 0), (second, 1), (second, 2),
-        (second, 3),
+        (front, 0), (front, 1), (front, 2), (first, 0), (front, 3), (first, 1), (hand_over, 0), (first, 2), (pass_on, 0, 1), (hand_over, 1), (first, 3), (pass_on, 1, 1), (hand_over, 2),
+        (pass_on, 2, 1), (hand_over, 3), (pass_on, 3, 1), (second, 0), (second, 1), (second, 2), (second, 3),
     )
-    for step, g in plan:
-        step(g)
+    for step, *at in plan:
+        step(*at)
     for g in range(QUADS):
         finish(g, seconds[g])
-    for groups in (halos, rims.values(), finals.values(), passed.values(), seconds.values()):
+    for copy in stores:
+        copy.wait()
+    hops = [list(copies.values()) for copies in firsts.values()]
+    for groups in (halos, rims.values(), hops, seconds.values()):
         for copies in groups:
             for copy in copies:
                 copy.wait_send()
 
 
 def hand_out(*refs):
-    for source, target in zip(refs[:3], refs[3:], strict=True):
-        target[...] = source[...]
+    sources, targets, held, sems = refs[:3], refs[3:6], refs[6:9], refs[9]
+    loads = [pltpu.make_async_copy(a, b, sems.at[0, i]) for i, (a, b) in enumerate(zip(sources, held))]
+    stores = [pltpu.make_async_copy(a, b, sems.at[1, i]) for i, (a, b) in enumerate(zip(held, targets))]
+    for copy in loads:
+        copy.start()
+    for load, store in zip(loads, stores):
+        load.wait()
+        store.start()
+    for copy in stores:
+        copy.wait()
 
 
 def per_device(queries, latent_kv, pair_blocks, pair_count, obs_count, cotangent):
@@ -404,8 +424,10 @@
             jax.ShapeDtypeStruct((1, 4, 2 * width), F32),
         ),
         in_specs=[hbm, hbm, smem, smem, smem, hbm],
-        out_specs=(vmem, vmem, vmem),
+        out_specs=(hbm, hbm, vmem),
         scratch_shapes=[
+            pltpu.VMEM((rows, width), BF16),
+            pltpu.VMEM((rows, width), BF16),
             pltpu.VMEM((rows, width), BF16),
             pltpu.VMEM((rows, width), BF16),
             pltpu.VMEM((H, WIN * BLOCK, rows), BF16),
@@ -416,10 +438,11 @@
             pltpu.VMEM((QUADS, 2, 32, 16, 128), BF16),
             pltpu.VMEM((QUADS, NY, NZ, 16, 128), BF16),
             pltpu.VMEM((QUADS, NZ - 1, NZ, 16, 128), BF16),
-            pltpu.VMEM((QUADS, 5, NZ, 16, 128), BF16),
+            pltpu.VMEM((QUADS, NZ, NZ, 16, 128), BF16),
             pltpu.VMEM((QUADS, NZ, 16, 128), BF16),
             pltpu.VMEM((QUADS, NZ - 1, 16, 128), BF16),
             dma((3,)),
+            dma((QUADS, 2)),
             dma((QUADS, 2, 2)),
             dma((QUADS, 2, 2)),
             dma((QUADS, 2)),
@@ -436,8 +459,10 @@
     return pl.pallas_call(
         hand_out,
         out_shape=tuple(jax.ShapeDtypeStruct(r.shape, r.dtype) for r in results),
-        in_specs=[vmem] * 3,
-        out_specs=(vmem,) * 3,
+        in_specs=[hbm] * 3,
+        out_specs=(hbm,) * 3,
+        scratch_shapes=[pltpu.VMEM(r.shape, r.dtype) for r in results] + [dma((2, 3))],
+        compiler_params=pltpu.CompilerParams(vmem_limit_bytes=60 * 1024 * 1024),
     )(*results)
 
 

time: 64.7 us -> 62.7 us (0.969)
  Pallas kernels: 63.3 us -> 61.7 us
    pallas_call x1, Pallas kernels: 61.1 us -> 59.7 us  [per_device(): pl.pallas_call(kernel, out_shape=(jax.ShapeDtypeStruct((rows, width), BF1...]
where the time goes in v3:
time: 62.7 us; the launch traced here: 62.5 us
  Pallas kernels  61.7 us (98%)
  between operations  0.8 us (1%)
    pallas_call x1, Pallas kernels, per_device(): pl.pallas_call(kernel, out_shape=(jax.ShapeDtypeStruct((rows, width), BF1...  59.7 us
    pallas_call x1, Pallas kernels, per_device(): pl.pallas_call(hand_out, out_shape=tuple((jax.ShapeDtypeStruct(r.shape, r...  2.06 us

profile of v3, /device:TPU:1, one launch (start us, length us, event | category | flops | bytes accessed | tf_op | source)
XLA Modules:
  0.0 62.5 jit_solution(6308400043552194831)
XLA Ops:
  0.6 59.7 %shard_map.85 = (bf16[256,1024]{1,0:T(8,128)(2,1)}, bf16[256,1024]{1,0:T(8,128)(2,1)}, f32[1,4,2048]{2,1,0:T(4,128)}) custom-call(bf16[256,1024]{1,0:T(8,128)(2,1)} %queries.1, bf16[1,384,2048]{2,1,0:T(8,128)(2,1)} %latent.1, s32[2,4]{1,0:T(2,128)} %blocks.1, s32[2]{0:T(128)} %pair_count.1, s32[2]{0:T(128)} %obs_count.1, bf16[256,1024]{1,0:T(8,128)(2,1)} %cotangent.1), custom_call_target="tpu_custom_call" | custom-call | tf_op jit(solution)/shard_map/pallas_call | solution.py:419
  60.3 2.1 %shard_map.86 = (bf16[256,1024]{1,0:T(8,128)(2,1)}, bf16[256,1024]{1,0:T(8,128)(2,1)}, f32[1,4,2048]{2,1,0:T(4,128)}) custom-call(bf16[256,1024]{1,0:T(8,128)(2,1)} %get-tuple-element.6.refs_0_, bf16[256,1024]{1,0:T(8,128)(2,1)} %get-tuple-element.7.refs_1_, f32[1,4,2048]{2,1,0:T(4,128)} %get-tuple-element.8.refs_2_), custom_call_target="tpu_custom_call" | custom-call | tf_op jit(solution)/shard_map/pallas_call | solution.py:459

commit v4 on v3

--- a/solution.py
+++ b/solution.py
@@ -22,10 +22,13 @@
 F32, BF16 = jnp.float32, jnp.bfloat16
 HALO_QUADS = ((0, 1), (1, 1), (2, 2))
 FIRST_AXIS = ("z", "y", "z", "y")
-RUNS = {
-    "y": ((1, 4, 3), (1, 2, 1), (-1, 3, 2), (-1, 1, 1)),
-    "z": ((1, 6, 5), (1, 4, 3), (1, 2, 1), (-1, 5, 4), (-1, 3, 2), (-1, 1, 1)),
-}
+TURN = (1, 1, -1, -1)
+RUNS = (
+    ((1, 6, 5), (1, 4, 3), (1, 2, 1), (-1, 5, 4), (-1, 3, 2), (-1, 1, 1)),
+    ((1, 4, 3), (1, 2, 1), (-1, 3, 2), (-1, 1, 1)),
+    ((1, 6, 5), (1, 4, 3), (1, 2, 1), (-1, 5, 4), (-1, 3, 2), (-1, 1, 1)),
+    ((1, 4, 3), (1, 2, 1), (-1, 3, 2), (-1, 1, 1)),
+)
 
 
 def dot(a, b):
@@ -278,10 +281,10 @@
         )
 
     def runs_of(g):
-        axis, turn = FIRST_AXIS[g], 1 if g < QUADS // 2 else -1
+        axis, turn = FIRST_AXIS[g], TURN[g]
         runs, at = [], 0
-        hops = sum(far - near for _, far, near in RUNS[axis])
-        for n, (sign, far, near) in enumerate(RUNS[axis]):
+        hops = sum(far - near for _, far, near in RUNS[g])
+        for n, (sign, far, near) in enumerate(RUNS[g]):
             runs.append((turn * sign, tuple(range(far, near - 1, -1)), at, hops + n))
             at += far - near
         return axis, runs, hops
@@ -381,8 +384,9 @@
         seconds[g] = start_second(g)
 
     plan = (
-        (front, 0), (front, 1), (front, 2), (first, 0), (front, 3), (first, 1), (hand_over, 0), (first, 2), (pass_on, 0, 1), (hand_over, 1), (first, 3), (pass_on, 1, 1), (hand_over, 2),
-        (pass_on, 2, 1), (hand_over, 3), (pass_on, 3, 1), (second, 0), (second, 1), (second, 2), (second, 3),
+        (front, 0), (front, 1), (front, 2), (first, 0), (front, 3), (first, 1), (hand_over, 0), (first, 2), (pass_on, 0, 1), (hand_over, 1),
+        (first, 3), (pass_on, 1, 1), (hand_over, 2), (pass_on, 2, 1), (hand_over, 3), (pass_on, 3, 1),
+        (second, 0), (second, 1), (second, 3), (second, 2),
     )
     for step, *at in plan:
         step(*at)

time: 62.7 us -> 61.4 us (0.979)
  the two profiles are of different devices: /device:TPU:1 before, /device:TPU:64 now
where the time goes in v4:
time: 61.4 us; the launch traced here: 61.2 us
  Pallas kernels  60.4 us (98%)
  between operations  0.8 us (1%)
    pallas_call x1, Pallas kernels, per_device(): pl.pallas_call(kernel, out_shape=(jax.ShapeDtypeStruct((rows, width), BF1...  58.3 us
    pallas_call x1, Pallas kernels, per_device(): pl.pallas_call(hand_out, out_shape=tuple((jax.ShapeDtypeStruct(r.shape, r...  2.06 us

profile of v4, /device:TPU:64, one launch (start us, length us, event | category | flops | bytes accessed | tf_op | source)
XLA Modules:
  0.0 61.2 jit_solution(15864649851892349797)
XLA Ops:
  0.6 58.3 %shard_map.85 = (bf16[256,1024]{1,0:T(8,128)(2,1)}, bf16[256,1024]{1,0:T(8,128)(2,1)}, f32[1,4,2048]{2,1,0:T(4,128)}) custom-call(bf16[256,1024]{1,0:T(8,128)(2,1)} %queries.1, bf16[1,384,2048]{2,1,0:T(8,128)(2,1)} %latent.1, s32[2,4]{1,0:T(2,128)} %blocks.1, s32[2]{0:T(128)} %pair_count.1, s32[2]{0:T(128)} %obs_count.1, bf16[256,1024]{1,0:T(8,128)(2,1)} %cotangent.1), custom_call_target="tpu_custom_call" | custom-call | tf_op jit(solution)/shard_map/pallas_call | solution.py:423
  59.0 2.1 %shard_map.86 = (bf16[256,1024]{1,0:T(8,128)(2,1)}, bf16[256,1024]{1,0:T(8,128)(2,1)}, f32[1,4,2048]{2,1,0:T(4,128)}) custom-call(bf16[256,1024]{1,0:T(8,128)(2,1)} %get-tuple-element.6.refs_0_, bf16[256,1024]{1,0:T(8,128)(2,1)} %get-tuple-element.7.refs_1_, f32[1,4,2048]{2,1,0:T(4,128)} %get-tuple-element.8.refs_2_), custom_call_target="tpu_custom_call" | custom-call | tf_op jit(solution)/shard_map/pallas_call | solution.py:463
